TPU v7x, 32 devices: a whole 2x2x4 slice. The times are simulated.
32 devices in a mesh: row: 16 (over z, y, x), col: 2 (over core).
Axes of the slice: x: 2, y: 2, z: 4, core: 2. Of those that a mesh axis runs over, the one named last changes fastest.
Arguments:
- gate_up: bfloat16 [4, 2, 14336, 4096], P(None, None, 'row', 'col'), may hold values from -0.09375 to 0.09375
- down_weight: bfloat16 [4, 4096, 14336], P(None, 'row', 'col'), may hold values from -0.046875 to 0.046875
- query_output: bfloat16 [4, 2, 4096, 4096], P(None, None, 'row', 'col'), may hold values from -0.09375 to 0.09375
- probe_gate: bfloat16 [4, 2, 16, 4096], P(None, None, None, 'col'), may hold values from -6 to 6
- probe_down: bfloat16 [4, 16, 14336], P(None, None, 'col'), may hold values from -6 to 6
- probe_query: bfloat16 [4, 2, 16, 4096], P(None, None, None, 'col'), may hold values from -6 to 6
Outputs:
- vector_gate: float32 [4, 2, 16, 4096], P(None, None, None, 'col')
- vector_down: float32 [4, 16, 14336], P(None, None, 'col')
- vector_query: float32 [4, 2, 16, 4096], P(None, None, None, 'col')
- sigma_gate: float32 [4, 2, 16], replicated
- sigma_down: float32 [4, 16], replicated
- sigma_query: float32 [4, 2, 16], replicated
All inputs are finite; a program needn't handle non-finite values.
Results may differ from a plain program's by a relative error of at most 0.0033.
Values may be sent and summed in bfloat16 or wider, within the bound.
A program may use at most 128 MiB of HBM per device.

v0:
```python
import jax
import jax.numpy as jnp
from jax import lax
from jax.sharding import PartitionSpec as P

ITERS = 2


epsilon = 1e-06


def body(gate_up, down_weight, query_output, probe_gate, probe_down, probe_query):
    row_count = lax.axis_size("row")
    col_count = lax.axis_size("col")
    weights = (gate_up, down_weight[:, None], query_output)
    vectors = (probe_gate, probe_down[:, None], probe_query)
    scaled_right = vectors
    spectral = None

    def left_factor(total, weight):
        return lax.rsqrt(total[..., None] / (weight.shape[2] * row_count) + epsilon)

    for turn in range(ITERS):
        partial_value = tuple(
            (
                jnp.einsum("lmoi,lmki->lmko", weight, vector, preferred_element_type=jnp.float32)
                for weight, vector in zip(weights, vectors)
            )
        )
        summed = lax.psum(partial_value, "col")
        squares = tuple((jnp.sum(piece * piece, axis=3) for piece in summed))
        totals = lax.psum(squares, "row")
        left_vecs = tuple((piece.astype(jnp.bfloat16) for piece in summed))
        right_partial = tuple(
            (
                jnp.einsum("lmoi,lmko->lmki", weight, left, preferred_element_type=jnp.float32)
                for weight, left in zip(weights, left_vecs)
            )
        )
        raw_sums = lax.psum(right_partial, "row")
        right_sums = tuple(
            (
                raw * left_factor(total, weight)
                for raw, total, weight in zip(raw_sums, totals, weights)
            )
        )
        right_squares = tuple((jnp.sum(piece * piece, axis=3) for piece in right_sums))
        right_totals = lax.psum(right_squares, "col")
        scaled_right = tuple(
            (
                piece * lax.rsqrt(total[..., None] / (piece.shape[3] * col_count) + epsilon)
                for piece, total in zip(right_sums, right_totals)
            )
        )
        spectral = tuple(
            (
                jnp.sqrt(total / (weight.shape[2] * row_count))
                for weight, total in zip(weights, right_totals)
            )
        )
        vectors = tuple((piece.astype(jnp.bfloat16) for piece in scaled_right))
    return (
        scaled_right[0],
        scaled_right[1][:, 0],
        scaled_right[2],
        spectral[0],
        spectral[1][:, 0],
        spectral[2],
    )


def solution(mesh):
    return jax.shard_map(
        body,
        mesh=mesh,
        in_specs=(
            P(None, None, "row", "col"),
            P(None, "row", "col"),
            P(None, None, "row", "col"),
            P(None, None, None, "col"),
            P(None, None, "col"),
            P(None, None, None, "col"),
        ),
        out_specs=(
            P(None, None, None, "col"),
            P(None, None, "col"),
            P(None, None, None, "col"),
            P(),
            P(),
            P(),
        ),
        check_vma=False,
    )
```

profile of v0, /device:TPU:0, one launch (start us, length us, event | category | flops | bytes accessed | tf_op | source)
XLA Modules:
  0.0 525.1 jit_solution(13970360872277524652)
XLA Ops:
  7.2 0.0 copy-start
  7.2 0.0 copy-start.10
  7.2 0.0 all-reduce.19.cloned.1.call-start
  7.2 1.1 copy-done
  8.4 9.8 %convolution_bitcast_fusion.3 = f32[4,1,16,256]{3,2,0,1:T(8,128)} fusion(bf16[4,16,7168]{2,1,0:T(8,128)(2,1)S(1)} %copy-done, bf16[4,256,7168]{2,1,0:T(8,128)(2,1)} %param.7), kind=kOutput, calls=%fused_computation.7 | convolution fusion | flops 234881024 | bytes 15663104 | tf_op jit(solution)/shard_map/lmoi,lmki->lmko/dot_general | solution.py:26
  18.2 2.9 fusion.23
  21.1 14.0 %fusion.22 = f32[4,2,16,896]{3,2,1,0:T(8,128)} fusion(bf16[4,2,16,2048]{3,2,1,0:T(8,128)(2,1)S(1)} %copy-done.13, bf16[4,2,896,2048]{3,2,1,0:T(8,128)(2,1)} %param.6), kind=kOutput, calls=%fused_computation.58 | convolution fusion | flops 469762048 | bytes 30343168 | tf_op jit(solution)/shard_map/lmoi,lmki->lmko/dot_general | solution.py:26
  35.2 0.0 all-reduce.19.cloned.1.call-update
  35.2 0.2 all-reduce.15.cloned.1.call-start
  35.4 21.7 %all-reduce.19.cloned.1.call-done = (f32[4,2,16,896]{3,2,1,0:T(8,128)}, f32[4,1,16,256]{3,2,0,1:T(8,128)}, f32[4,2,16,256]{3,2,1,0:T(8,128)}) async-done(((f32[4,2,16,896]{3,2,1,0:T(8,128)}, f32[4,1,16,256]{3,2,0,1:T(8,128)}, f32[4,2,16,256]{3,2,1,0:T(8,128)}), (f32[4,2,16,896]{3,2,1,0:T(8,128)}, f32[4,1,16,256]{3,2,0,1:T(8,128)}, f32[4,2,16,256]{3,2,1,0:T(8,128)})) %all-reduce.19.cloned.1.call-update) | async-done | bytes 655376 | tf_op jit(solution)/shard_map/psum | solution.py:30
  57.2 14.5 %fusion.12 = f32[4,2,16,2048]{3,2,1,0:T(8,128)} fusion(bf16[4,2,896,2048]{3,2,1,0:T(8,128)(2,1)} %param.6, f32[4,2,16,896]{3,2,1,0:T(8,128)} %get-tuple-element.27), kind=kOutput, calls=%fused_computation.29 | convolution fusion | flops 469876736 | bytes 30867456 | tf_op jit(solution)/shard_map/lmoi,lmko->lmki/dot_general | solution.py:36
  71.6 5.6 %fusion.16 = f32[4,2,16,2048]{3,2,1,0:T(8,128)} fusion(bf16[4,2,256,2048]{3,2,1,0:T(8,128)(2,1)} %param.8, f32[4,2,16,256]{3,2,1,0:T(8,128)S(1)} %copy-done.11), kind=kOutput, calls=%fused_computation.35 | convolution fusion | flops 134250496 | bytes 9568256 | tf_op jit(solution)/shard_map/lmoi,lmko->lmki/dot_general | solution.py:36
  77.2 8.5 %convolution_bitcast_fusion.1 = f32[4,1,16,7168]{3,2,0,1:T(8,128)} fusion(bf16[4,256,7168]{2,1,0:T(8,128)(2,1)} %param.7, f32[4,1,16,256]{3,2,0,1:T(8,128)S(1)} %copy-done.8), kind=kOutput, calls=%fused_computation.1 | convolution fusion | flops 234897408 | bytes 16580608 | tf_op jit(solution)/shard_map/lmoi,lmko->lmki/dot_general | solution.py:36
  85.7 0.0 all-reduce.15.cloned.1.call-update
  85.7 0.0 all-reduce.17.cloned.1.call-start
  85.8 0.1 multiply_reduce_fusion.11
  85.9 0.1 multiply_reduce_fusion.9
  86.0 0.1 multiply_reduce_fusion.7
  86.1 79.3 %all-reduce.1 = (f32[4,2,16]{2,1,0:T(2,128)S(1)}, f32[4,1,16]{2,0,1:T(4,128)S(1)}, f32[4,2,16]{2,1,0:T(2,128)S(1)}) all-reduce(f32[4,2,16]{2,1,0:T(2,128)S(1)} %multiply_reduce_fusion.7, f32[4,1,16]{2,0,1:T(4,128)S(1)} %bitcast.50, f32[4,2,16]{2,1,0:T(2,128)S(1)} %multiply_reduce_fusion.9), channel_id=1, replica_groups=mesh['row'=16,'col'=2] {'row'}, use_global_device_ids=true, to_apply=%region_3.0 | all-reduce | flops 320 | bytes 2560 | tf_op jit(solution)/shard_map/psum | solution.py:32
  165.5 86.2 %all-reduce.15.cloned.1.call-done = (f32[4,2,16,2048]{3,2,1,0:T(8,128)}, f32[4,1,16,7168]{3,2,0,1:T(8,128)}, f32[4,2,16,2048]{3,2,1,0:T(8,128)}) async-done(((f32[4,2,16,2048]{3,2,1,0:T(8,128)}, f32[4,1,16,7168]{3,2,0,1:T(8,128)}, f32[4,2,16,2048]{3,2,1,0:T(8,128)}), (f32[4,2,16,2048]{3,2,1,0:T(8,128)}, f32[4,1,16,7168]{3,2,0,1:T(8,128)}, f32[4,2,16,2048]{3,2,1,0:T(8,128)})) %all-reduce.15.cloned.1.call-update) | async-done | bytes 3932176 | tf_op jit(solution)/shard_map/psum | solution.py:40
  251.7 1.8 multiply_reduce_fusion.1
  253.5 1.9 multiply_reduce_fusion.3
  255.4 3.3 all-reduce.5
  258.7 14.5 %fusion.4 = f32[4,2,16,896]{3,2,1,0:T(8,128)} fusion(bf16[4,2,896,2048]{3,2,1,0:T(8,128)(2,1)} %param.6, f32[4,2,16,2048]{3,2,1,0:T(8,128)} %get-tuple-element.15, f32[4,2,16]{2,1,0:T(2,128)S(1)} %add_rsqrt_fusion.6, f32[4,2,16]{2,1,0:T(2,128)S(1)} %add_rsqrt_fusion.7), kind=kOutput, calls=%fused_computation.19 | convolution fusion | flops 470548480 | bytes 30868480 | tf_op jit(solution)/shard_map/lmoi,lmki->lmko/dot_general | solution.py:26
  273.2 9.8 %convolution_bitcast_fusion.2 = f32[4,1,16,256]{3,2,0,1:T(8,128)} fusion(bf16[4,256,7168]{2,1,0:T(8,128)(2,1)} %param.7, f32[4,1,16,7168]{3,2,0,1:T(8,128)S(1)} %copy-done.3, f32[4,16]{1,0:T(4,128)S(1)} %rsqrt_bitcast_fusion.2, f32[4,16]{1,0:T(4,128)S(1)} %rsqrt_bitcast_fusion.3), kind=kOutput, calls=%fused_computation.6 | convolution fusion | flops 236257280 | bytes 16581120 | tf_op jit(solution)/shard_map/lmoi,lmki->lmko/dot_general | solution.py:26
  283.0 6.3 %fusion.5 = f32[4,2,16,256]{3,2,1,0:T(8,128)} fusion(bf16[4,2,256,2048]{3,2,1,0:T(8,128)(2,1)} %param.8, f32[4,2,16,2048]{3,2,1,0:T(8,128)S(1)} %copy-done.4, f32[4,2,16]{2,1,0:T(2,128)S(1)} %add_rsqrt_fusion.2, f32[4,2,16]{2,1,0:T(2,128)S(1)} %add_rsqrt_fusion.3), kind=kOutput, calls=%fused_computation.20 | convolution fusion | flops 135004160 | bytes 9569280 | tf_op jit(solution)/shard_map/lmoi,lmki->lmko/dot_general | solution.py:26
  289.4 0.0 all-reduce.17.cloned.1.call-update
  289.4 0.3 all-reduce.13.cloned.1.call-start
  289.7 18.0 %all-reduce.17.cloned.1.call-done = (f32[4,2,16,896]{3,2,1,0:T(8,128)}, f32[4,1,16,256]{3,2,0,1:T(8,128)}, f32[4,2,16,256]{3,2,1,0:T(8,128)}) async-done(((f32[4,2,16,896]{3,2,1,0:T(8,128)}, f32[4,1,16,256]{3,2,0,1:T(8,128)}, f32[4,2,16,256]{3,2,1,0:T(8,128)}), (f32[4,2,16,896]{3,2,1,0:T(8,128)}, f32[4,1,16,256]{3,2,0,1:T(8,128)}, f32[4,2,16,256]{3,2,1,0:T(8,128)})) %all-reduce.17.cloned.1.call-update) | async-done | bytes 655376 | tf_op jit(solution)/shard_map/psum | solution.py:30
  307.7 14.5 %fusion.10 = f32[4,2,16,2048]{3,2,1,0:T(8,128)} fusion(bf16[4,2,896,2048]{3,2,1,0:T(8,128)(2,1)} %param.6, f32[4,2,16,896]{3,2,1,0:T(8,128)} %get-tuple-element.24), kind=kOutput, calls=%fused_computation.27 | convolution fusion | flops 469876736 | bytes 30867456 | tf_op jit(solution)/shard_map/lmoi,lmko->lmki/dot_general | solution.py:36
  322.1 5.6 %fusion.14 = f32[4,2,16,2048]{3,2,1,0:T(8,128)} fusion(bf16[4,2,256,2048]{3,2,1,0:T(8,128)(2,1)} %param.8, f32[4,2,16,256]{3,2,1,0:T(8,128)S(1)} %copy-done.12), kind=kOutput, calls=%fused_computation.33 | convolution fusion | flops 134250496 | bytes 9568256 | tf_op jit(solution)/shard_map/lmoi,lmko->lmki/dot_general | solution.py:36
  327.7 8.5 %convolution_bitcast_fusion = f32[4,1,16,7168]{3,2,0,1:T(8,128)} fusion(bf16[4,256,7168]{2,1,0:T(8,128)(2,1)} %param.7, f32[4,1,16,256]{3,2,0,1:T(8,128)S(1)} %copy-done.9), kind=kOutput, calls=%fused_computation | convolution fusion | flops 234897408 | bytes 16580608 | tf_op jit(solution)/shard_map/lmoi,lmko->lmki/dot_general | solution.py:36
  336.3 0.0 all-reduce.13.cloned.1.call-update
  336.3 0.1 multiply_reduce_fusion.10
  336.4 0.1 multiply_reduce_fusion.8
  336.5 0.1 multiply_reduce_fusion.6
  336.6 79.1 %all-reduce = (f32[4,2,16]{2,1,0:T(2,128)S(1)}, f32[4,1,16]{2,0,1:T(4,128)S(1)}, f32[4,2,16]{2,1,0:T(2,128)S(1)}) all-reduce(f32[4,2,16]{2,1,0:T(2,128)S(1)} %multiply_reduce_fusion.6, f32[4,1,16]{2,0,1:T(4,128)S(1)} %bitcast.51, f32[4,2,16]{2,1,0:T(2,128)S(1)} %multiply_reduce_fusion.8), channel_id=1, replica_groups=mesh['row'=16,'col'=2] {'row'}, use_global_device_ids=true, to_apply=%region_9.0 | all-reduce | flops 320 | bytes 2560 | tf_op jit(solution)/shard_map/psum | solution.py:32
  415.7 86.4 %all-reduce.13.cloned.1.call-done = (f32[4,2,16,2048]{3,2,1,0:T(8,128)}, f32[4,1,16,7168]{3,2,0,1:T(8,128)}, f32[4,2,16,2048]{3,2,1,0:T(8,128)}) async-done(((f32[4,2,16,2048]{3,2,1,0:T(8,128)}, f32[4,1,16,7168]{3,2,0,1:T(8,128)}, f32[4,2,16,2048]{3,2,1,0:T(8,128)}), (f32[4,2,16,2048]{3,2,1,0:T(8,128)}, f32[4,1,16,7168]{3,2,0,1:T(8,128)}, f32[4,2,16,2048]{3,2,1,0:T(8,128)})) %all-reduce.13.cloned.1.call-update) | async-done | bytes 3932176 | tf_op jit(solution)/shard_map/psum | solution.py:40
  502.1 1.9 multiply_reduce_fusion
  504.0 1.5 multiply_reduce_fusion.4
  505.5 1.5 multiply_reduce_fusion.2
  507.0 3.3 all-reduce.4
  510.3 0.6 multiply_sqrt_fusion
  510.9 2.4 multiply_multiply_fusion.1
  513.3 0.6 sqrt_bitcast_fusion
  513.9 2.9 multiply_bitcast_fusion
  516.8 0.6 multiply_sqrt_fusion.1
  517.4 1.2 multiply_multiply_fusion
  (34 shorter events, 0.1 us)
Async XLA Ops:
  7.2 1.2 copy-start
  7.2 11.0 %copy-start.10 = (bf16[4,2,16,2048]{3,2,1,0:T(8,128)(2,1)S(1)}, bf16[4,2,16,2048]{3,2,1,0:T(8,128)(2,1)}, u32[]{:S(2)}) copy-start(bf16[4,2,16,2048]{3,2,1,0:T(8,128)(2,1)} %param.11) | copy-start | bytes 1572868
  7.2 50.0 %all-reduce.19.cloned.1.call-start = ((), (), s32[]{:S(2)}) async-start(), calls=%async_computation.3 | async-start | bytes 1310720 | tf_op jit(solution)/shard_map/psum | solution.py:30
  8.4 9.9 %copy-start.2 = (bf16[4,2,256,2048]{3,2,1,0:T(8,128)(2,1)S(1)}, bf16[4,2,256,2048]{3,2,1,0:T(8,128)(2,1)}, u32[]{:S(2)}) copy-start(bf16[4,2,256,2048]{3,2,1,0:T(8,128)(2,1)} %param.8) | copy-start | bytes 25165828
  18.2 2.9 copy-start.13
  35.2 216.4 %all-reduce.15.cloned.1.call-start = ((), (), s32[]{:S(2)}) async-start(), calls=%async_computation.1 | async-start | bytes 7864320 | tf_op jit(solution)/shard_map/psum | solution.py:40
  57.2 14.5 %copy-start.11 = (f32[4,2,16,256]{3,2,1,0:T(8,128)S(1)}, f32[4,2,16,256]{3,2,1,0:T(8,128)}, u32[]{:S(2)}) copy-start(f32[4,2,16,256]{3,2,1,0:T(8,128)} %get-tuple-element.29) | copy-start | bytes 393220
  71.6 5.6 %copy-start.8 = (f32[4,1,16,256]{3,2,0,1:T(8,128)S(1)}, f32[4,1,16,256]{3,2,0,1:T(8,128)}, u32[]{:S(2)}) copy-start(f32[4,1,16,256]{3,2,0,1:T(8,128)} %get-tuple-element.28) | copy-start | bytes 196612
  77.2 8.8 %copy-start.6 = (f32[4,2,16,896]{3,2,1,0:T(8,128)S(1)}, f32[4,2,16,896]{3,2,1,0:T(8,128)}, u32[]{:S(2)}) copy-start(f32[4,2,16,896]{3,2,1,0:T(8,128)} %get-tuple-element.27) | copy-start | bytes 1376260
  85.7 221.9 %all-reduce.17.cloned.1.call-start = ((), (), s32[]{:S(2)}) async-start(), calls=%async_computation.2 | async-start | bytes 1310720 | tf_op jit(solution)/shard_map/psum | solution.py:30
  258.7 14.5 %copy-start.3 = (f32[4,1,16,7168]{3,2,0,1:T(8,128)S(1)}, f32[4,1,16,7168]{3,2,0,1:T(8,128)}, u32[]{:S(2)}) copy-start(f32[4,1,16,7168]{3,2,0,1:T(8,128)} %get-tuple-element.16) | copy-start | bytes 5505028
  273.2 9.8 %copy-start.4 = (f32[4,2,16,2048]{3,2,1,0:T(8,128)S(1)}, f32[4,2,16,2048]{3,2,1,0:T(8,128)}, u32[]{:S(2)}) copy-start(f32[4,2,16,2048]{3,2,1,0:T(8,128)} %get-tuple-element.17) | copy-start | bytes 3145732
  289.4 212.7 %all-reduce.13.cloned.1.call-start = ((), (), s32[]{:S(2)}) async-start(), calls=%async_computation | async-start | bytes 7864320 | tf_op jit(solution)/shard_map/psum | solution.py:40
  307.7 14.5 %copy-start.12 = (f32[4,2,16,256]{3,2,1,0:T(8,128)S(1)}, f32[4,2,16,256]{3,2,1,0:T(8,128)}, u32[]{:S(2)}) copy-start(f32[4,2,16,256]{3,2,1,0:T(8,128)} %get-tuple-element.26) | copy-start | bytes 393220
  322.1 5.6 %copy-start.9 = (f32[4,1,16,256]{3,2,0,1:T(8,128)S(1)}, f32[4,1,16,256]{3,2,0,1:T(8,128)}, u32[]{:S(2)}) copy-start(f32[4,1,16,256]{3,2,0,1:T(8,128)} %get-tuple-element.25) | copy-start | bytes 196612
  327.7 8.8 %copy-start.7 = (f32[4,2,16,896]{3,2,1,0:T(8,128)S(1)}, f32[4,2,16,896]{3,2,1,0:T(8,128)}, u32[]{:S(2)}) copy-start(f32[4,2,16,896]{3,2,1,0:T(8,128)} %get-tuple-element.24) | copy-start | bytes 1376260
  327.7 190.9 %copy-start.1 = (bf16[4,16,7168]{2,1,0:T(8,128)(2,1)S(1)}, bf16[4,16,7168]{2,1,0:T(8,128)(2,1)}, u32[]{:S(2)}) copy-start(bf16[4,16,7168]{2,1,0:T(8,128)(2,1)} %param.10) | copy-start | bytes 2752516
  502.1 15.3 %copy-start.5 = (f32[4,2,16,2048]{3,2,1,0:T(8,128)S(1)}, f32[4,2,16,2048]{3,2,1,0:T(8,128)}, u32[]{:S(2)}) copy-start(f32[4,2,16,2048]{3,2,1,0:T(8,128)} %get-tuple-element.14) | copy-start | bytes 3145732
Sparse Core Ops, SparseCore 0:
  35.3 21.7 all-reduce.18
  85.9 165.7 all-reduce.14
  289.5 18.1 all-reduce.16
  336.4 165.6 all-reduce.12
where the time goes:
time: 526 us; the launch traced here: 525 us
  waiting for transfers between devices  212 us (40%)
  blocking collectives  165 us (31%)
  matrix products  115 us (22%)
  other arithmetic  17.6 us (3%)
  between operations  13.9 us (3%)
    psum x2, waiting for transfers between devices, body(): raw_sums = lax.psum(right_partial, 'row')  173 us
    psum x2, blocking collectives, body(): totals = lax.psum(squares, 'row')  158 us
    dot_general x6, matrix products, body(): jnp.einsum('lmoi,lmki->lmko', weight, vector, preferred_element_type=jnp....  57.4 us
    dot_general x6, matrix products, body(): jnp.einsum('lmoi,lmko->lmki', weight, left, preferred_element_type=jnp.fl...  57.1 us
    psum x2, waiting for transfers between devices, body(): summed = lax.psum(partial_value, 'col')  39.7 us
  transfers between devices with their start and end apart: 4, of which 4 were waited for; matrix products, arithmetic and copies ran while one was open for 0% of the time, Pallas kernels for 0%

commit v1 on v0

--- a/solution.py
+++ b/solution.py
@@ -1,6 +1,11 @@
+import functools
+import math
+
 import jax
 import jax.numpy as jnp
 from jax import lax
+from jax.experimental import pallas as pl
+from jax.experimental.pallas import tpu as pltpu
 from jax.sharding import PartitionSpec as P
 
 ITERS = 2
@@ -8,8 +13,373 @@
 
 epsilon = 1e-06
 
-
-def body(gate_up, down_weight, query_output, probe_gate, probe_down, probe_query):
+LANES = 128
+LOW = 4
+LEAST = 4096
+VMEM_BYTES = 64 * 2**20
+MESH = pl.DeviceIdType.MESH
+
+
+def batch_of(count, width, rows):
+    for size in range(1, count + 1):
+        total = size * width
+        if count % size or total < LEAST or total % (rows * LANES):
+            continue
+        piece = total // rows
+        if width % piece == 0 and rows % size == 0:
+            return size
+    return None
+
+
+class Group:
+    def __init__(self, count, out, width, probes, rows, first):
+        self.count, self.out, self.width, self.first = count, out, width, first
+        self.size = batch_of(count, width, rows)
+        self.batches = count // self.size
+        self.piece = self.size * width // rows
+        self.per = rows // self.size
+
+
+def kernel(sizes, rows, probes, *refs):
+    low_n, high_n = LOW, rows // LOW
+    kinds = len(sizes)
+    refs = list(refs)
+
+    def take(n):
+        out = refs[:n]
+        del refs[:n]
+        return out
+
+    w_hbm, p_hbm, v_out = take(kinds), take(kinds), take(kinds)
+    scale_out, sigma_out = take(2)
+    (ws, vs, rss, prs, lss, lrs, css, crs) = (take(kinds) for _ in range(8))
+    wsem, vsem, csem, rsem = (take(kinds) for _ in range(4))
+    psend, precv, lsend, lrecv = (take(kinds) for _ in range(4))
+    qsend, qrecv, tsend, trecv = (take(kinds) for _ in range(4))
+    ltp, ltl, rtc, scale_ref, left_ref, ltsem, llsem, rtsem = take(8)
+
+    row, col = lax.axis_index("row"), lax.axis_index("col")
+    low, high = lax.rem(row, low_n), row // low_n
+    plane = [lax.rem(low + k, low_n) for k in range(1, low_n)]
+    line = [lax.rem(high + k, high_n) for k in range(1, high_n)]
+
+    def at_plane(q):
+        return (high * low_n + q, col)
+
+    def at_line(h):
+        return (h * low_n + low, col)
+
+    across = (row, 1 - col)
+
+    def remote(src, dst, send, recv, device):
+        return pltpu.make_async_remote_copy(
+            src_ref=src, dst_ref=dst, send_sem=send, recv_sem=recv,
+            device_id=device, device_id_type=MESH)
+
+    lane = lax.broadcasted_iota(jnp.int32, (probes, LANES), 1)
+
+    def load_w(g, m):
+        return pltpu.make_async_copy(w_hbm[g].at[m], ws[g].at[m], wsem[g].at[m])
+
+    order = [(g, b) for g in reversed(range(kinds)) for b in range(sizes[g].batches)]
+
+    for g, b in order:
+        s = sizes[g]
+
+        @pl.loop(0, s.size)
+        def _(i, g=g, b=b, s=s):
+            m = b * s.size + i
+            for j in range(s.per):
+                pltpu.make_async_copy(
+                    p_hbm[g].at[m, :, pl.ds(j * s.piece, s.piece)],
+                    vs[g].at[b, i * s.per + j], vsem[g].at[b]).start()
+            load_w(g, m).start()
+
+    barrier = pltpu.get_barrier_semaphore()
+    peers = [across] + [at_plane(q) for q in plane] + [at_line(h) for h in line]
+    for peer in peers:
+        pl.semaphore_signal(barrier, inc=1, device_id=peer, device_id_type=MESH)
+    pl.semaphore_wait(barrier, len(peers))
+
+    scale_ref[...] = jnp.ones_like(scale_ref)
+
+    def pick(array, m):
+        return jnp.sum(jnp.where(lane == m, array, 0.0), axis=1, keepdims=True)
+
+    def cross(g, m):
+        return remote(css[g].at[m], crs[g].at[m], csem[g].at[m], rsem[g].at[m], across)
+
+    def stage_left(turn, g, b):
+        s = sizes[g]
+
+        @pl.when(turn == 0)
+        def _():
+            pltpu.make_async_copy(vs[g].at[b], vs[g].at[b], vsem[g].at[b]).wait()
+
+        @pl.loop(0, s.size)
+        def _(i):
+            m = b * s.size + i
+
+            @pl.when(turn == 0)
+            def _():
+                load_w(g, m).wait()
+
+            total = None
+            for j in range(s.per):
+                term = lax.dot_general(
+                    vs[g][b, i * s.per + j],
+                    ws[g][m, :, pl.ds(j * s.piece, s.piece)],
+                    (((1,), (1,)), ((), ())), preferred_element_type=jnp.float32)
+                total = term if total is None else total + term
+            css[g][m] = total
+            cross(g, m).start()
+
+    def plane_copy(g, b, k):
+        q = plane[k]
+        return remote(rss[g].at[b, pl.ds(q * high_n, high_n)], prs[g].at[b, low],
+                      psend[g].at[b, k], precv[g].at[b, low], at_plane(q))
+
+    def stage_right(g, b):
+        s = sizes[g]
+
+        @pl.loop(0, s.size)
+        def _(i):
+            m = b * s.size + i
+            cross(g, m).wait_recv()
+            left = (css[g][m] + crs[g][m]) * pick(scale_ref[...], s.first + m)
+            square = jnp.sum(left * left, axis=1, keepdims=True)
+            left_ref[...] = jnp.where(lane == s.first + m, square, left_ref[...])
+            left = left.astype(jnp.bfloat16)
+            for j in range(s.per):
+                rss[g][b, i * s.per + j] = jnp.dot(
+                    left, ws[g][m, :, pl.ds(j * s.piece, s.piece)],
+                    preferred_element_type=jnp.float32).astype(jnp.bfloat16)
+
+        for k in range(low_n - 1):
+            plane_copy(g, b, k).start()
+
+    def line_copy(g, b, k):
+        h = line[k]
+        return remote(lss[g].at[b, h], lrs[g].at[b, high],
+                      lsend[g].at[b, k], lrecv[g].at[b, high], at_line(h))
+
+    def stage_plane(g, b):
+        for q in plane:
+            pltpu.make_async_copy(prs[g].at[b, q], prs[g].at[b, q], precv[g].at[b, q]).wait()
+        for z in range(high_n):
+            total = rss[g][b, low * high_n + z].astype(jnp.float32)
+            for q in plane:
+                total = total + prs[g][b, q, z].astype(jnp.float32)
+            lss[g][b, z] = total
+        for k in range(high_n - 1):
+            line_copy(g, b, k).start()
+
+    def spread_line(g, b, k):
+        own = vs[g].at[b, row_piece]
+        return remote(own, own, qsend[g].at[b, k], qrecv[g].at[b, high], at_line(line[k]))
+
+    row_piece = low * high_n + high
+
+    def stage_line(g, b):
+        total = lss[g][b, high]
+        for h in line:
+            pltpu.make_async_copy(lrs[g].at[b, h], lrs[g].at[b, h], lrecv[g].at[b, h]).wait()
+        for h in line:
+            total = total + lrs[g][b, h]
+        vs[g][b, row_piece] = total.astype(jnp.bfloat16)
+        for k in range(high_n - 1):
+            spread_line(g, b, k).start()
+
+    def spread_plane(g, b, k):
+        own = vs[g].at[b, pl.ds(low * high_n, high_n)]
+        return remote(own, own, tsend[g].at[b, k], trecv[g].at[b, low], at_plane(plane[k]))
+
+    def stage_spread(g, b):
+        for h in line:
+            part = vs[g].at[b, low * high_n + h]
+            pltpu.make_async_copy(part, part, qrecv[g].at[b, h]).wait()
+        for k in range(low_n - 1):
+            spread_plane(g, b, k).start()
+
+    def stage_last(g, b):
+        s = sizes[g]
+        for q in plane:
+            part = vs[g].at[b, pl.ds(q * high_n, high_n)]
+            pltpu.make_async_copy(part, part, trecv[g].at[b, q]).wait()
+        for i in range(s.size):
+            total = None
+            for j in range(s.per):
+                part = vs[g][b, i * s.per + j].astype(jnp.float32)
+                part = jnp.sum(part * part, axis=1, keepdims=True)
+                total = part if total is None else total + part
+            m = s.first + b * s.size + i
+            rtc[col] = jnp.where(lane == m, total, rtc[col])
+
+    def left_plane(k):
+        return remote(ltp.at[low], ltp.at[low], ltsem.at[0, k], ltsem.at[1, low], at_plane(plane[k]))
+
+    def left_line(k):
+        return remote(ltl.at[high], ltl.at[high], llsem.at[0, k], llsem.at[1, high], at_line(line[k]))
+
+    def right_across():
+        return remote(rtc.at[col], rtc.at[col], rtsem.at[0], rtsem.at[1], across)
+
+    def per_matrix(values):
+        out = jnp.full((probes, LANES), 1.0, jnp.float32)
+        for s, value in zip(sizes, values):
+            out = jnp.where(lane >= s.first, jnp.float32(value), out)
+        return out
+
+    outs = per_matrix([s.out * rows for s in sizes])
+    ins = per_matrix([s.width * 2 for s in sizes])
+
+    @pl.loop(0, ITERS)
+    def _(turn):
+        rtc[col] = jnp.zeros((probes, LANES), jnp.float32)
+        left_ref[...] = jnp.zeros_like(left_ref)
+        count = len(order)
+        for step in range(count + 5):
+            if step < count:
+                stage_left(turn, *order[step])
+            if 0 <= step - 1 < count:
+                stage_right(*order[step - 1])
+            if step == count:
+                ltp[low] = left_ref[...]
+                for k in range(low_n - 1):
+                    left_plane(k).start()
+            if 0 <= step - 3 < count:
+                stage_plane(*order[step - 3])
+            if step == count + 2:
+                for q in plane:
+                    pltpu.make_async_copy(ltp.at[q], ltp.at[q], ltsem.at[1, q]).wait()
+                total = ltp[0]
+                for q in range(1, low_n):
+                    total = total + ltp[q]
+                ltl[high] = total
+                for k in range(high_n - 1):
+                    left_line(k).start()
+            if 0 <= step - 4 < count:
+                stage_line(*order[step - 4])
+            if 0 <= step - 5 < count:
+                stage_spread(*order[step - 5])
+        for g, b in order:
+            stage_last(g, b)
+        right_across().start()
+        for h in line:
+            pltpu.make_async_copy(ltl.at[h], ltl.at[h], llsem.at[1, h]).wait()
+        total = ltl[0]
+        for h in range(1, high_n):
+            total = total + ltl[h]
+        factor = lax.rsqrt(total / outs + epsilon)
+        right_across().wait_send()
+        other = rtc.at[1 - col]
+        pltpu.make_async_copy(other, other, rtsem.at[1]).wait()
+        right_total = (rtc[0] + rtc[1]) * factor * factor
+        scale_ref[...] = factor * lax.rsqrt(right_total / ins + epsilon)
+        sigma_out[...] = jnp.sqrt(right_total / outs)
+        for k in range(low_n - 1):
+            left_plane(k).wait_send()
+        for k in range(high_n - 1):
+            left_line(k).wait_send()
+        for g, b in order:
+            s = sizes[g]
+            for i in range(s.size):
+                cross(g, b * s.size + i).wait_send()
+            for k in range(low_n - 1):
+                plane_copy(g, b, k).wait_send()
+                spread_plane(g, b, k).wait_send()
+            for k in range(high_n - 1):
+                line_copy(g, b, k).wait_send()
+                spread_line(g, b, k).wait_send()
+
+    scale_out[...] = scale_ref[...]
+    for g in range(kinds):
+        pltpu.make_async_copy(vs[g], v_out[g], vsem[g].at[0]).start()
+    for g in range(kinds):
+        pltpu.make_async_copy(vs[g], v_out[g], vsem[g].at[0]).wait()
+
+
+def fused(gate_up, down_weight, query_output, probe_gate, probe_down, probe_query):
+    rows = lax.axis_size("row")
+    high_n = rows // LOW
+    weights = [w.reshape((-1,) + w.shape[-2:]) for w in (gate_up, down_weight, query_output)]
+    starts = [p.reshape((-1,) + p.shape[-2:]) for p in (probe_gate, probe_down, probe_query)]
+    probes = starts[0].shape[1]
+    sizes, first = [], 0
+    for w in weights:
+        sizes.append(Group(w.shape[0], w.shape[1], w.shape[2], probes, rows, first))
+        first += w.shape[0]
+
+    def each(make):
+        return [make(s) for s in sizes]
+
+    def vmem(dtype, shape_of):
+        return each(lambda s: pltpu.VMEM(shape_of(s), dtype))
+
+    def sems(shape_of):
+        return each(lambda s: pltpu.SemaphoreType.DMA(shape_of(s)))
+
+    bf, f32 = jnp.bfloat16, jnp.float32
+    scratch = (
+        vmem(bf, lambda s: (s.count, s.out, s.width))
+        + vmem(bf, lambda s: (s.batches, rows, probes, s.piece))
+        + vmem(bf, lambda s: (s.batches, rows, probes, s.piece))
+        + vmem(bf, lambda s: (s.batches, LOW, high_n, probes, s.piece))
+        + vmem(f32, lambda s: (s.batches, high_n, probes, s.piece))
+        + vmem(f32, lambda s: (s.batches, high_n, probes, s.piece))
+        + vmem(f32, lambda s: (s.count, probes, s.out))
+        + vmem(f32, lambda s: (s.count, probes, s.out))
+        + sems(lambda s: (s.count,))
+        + sems(lambda s: (s.batches,))
+        + sems(lambda s: (s.count,))
+        + sems(lambda s: (s.count,))
+    )
+    for _ in range(2):
+        for n in (LOW, LOW, high_n, high_n) if _ == 0 else (high_n, high_n, LOW, LOW):
+            scratch += sems(lambda s: (s.batches, n))
+    small = (probes, LANES)
+    scratch += [
+        pltpu.VMEM((LOW,) + small, f32),
+        pltpu.VMEM((high_n,) + small, f32),
+        pltpu.VMEM((2,) + small, f32),
+        pltpu.VMEM(small, f32),
+        pltpu.VMEM(small, f32),
+        pltpu.SemaphoreType.DMA((2, LOW)),
+        pltpu.SemaphoreType.DMA((2, high_n)),
+        pltpu.SemaphoreType.DMA((2,)),
+    ]
+    work = sum(math.prod(w.shape) for w in weights)
+    *vectors, scale, sigma = pl.pallas_call(
+        functools.partial(kernel, sizes, rows, probes),
+        out_shape=each(lambda s: jax.ShapeDtypeStruct((s.batches, rows, probes, s.piece), bf))
+        + [jax.ShapeDtypeStruct(small, f32)] * 2,
+        in_specs=[pl.BlockSpec(memory_space=pl.ANY)] * 6,
+        out_specs=[pl.BlockSpec(memory_space=pl.ANY)] * 3
+        + [pl.BlockSpec(memory_space=pltpu.VMEM)] * 2,
+        scratch_shapes=scratch,
+        cost_estimate=pl.CostEstimate(
+            flops=4 * ITERS * probes * work, bytes_accessed=2 * work, transcendentals=0),
+        compiler_params=pltpu.CompilerParams(
+            collective_id=0, has_side_effects=True, vmem_limit_bytes=VMEM_BYTES),
+    )(*weights, *starts)
+    outs, sigmas = [], []
+    for s, vector, start in zip(sizes, vectors, (probe_gate, probe_down, probe_query)):
+        mine = scale[:, s.first : s.first + s.count].T
+        value = vector.reshape(s.count, s.per, probes, s.piece).astype(f32) * mine[:, None, :, None]
+        outs.append(value.transpose(0, 2, 1, 3).reshape(start.shape))
+        sigmas.append(sigma[:, s.first : s.first + s.count].T.reshape(start.shape[:-1]))
+    return (*outs, *sigmas)
+
+
+def fits(*arrays):
+    rows, cols = lax.axis_size("row"), lax.axis_size("col")
+    weights = arrays[: len(arrays) // 2]
+    held = sum(2 * math.prod(w.shape) for w in weights)
+    even = all(batch_of(math.prod(w.shape[:-2]), w.shape[-1], rows) for w in weights)
+    return cols == 2 and rows % LOW == 0 and even and held < 0.8 * VMEM_BYTES
+
+
+def plain(gate_up, down_weight, query_output, probe_gate, probe_down, probe_query):
     row_count = lax.axis_size("row")
     col_count = lax.axis_size("col")
     weights = (gate_up, down_weight[:, None], query_output)
@@ -69,6 +439,10 @@
     )
 
 
+def body(*arrays):
+    return (fused if fits(*arrays) else plain)(*arrays)
+
+
 def solution(mesh):
     return jax.shard_map(
         body,

time: 526 us -> 140 us (0.27)
  waiting for transfers between devices: 212 us -> 0 us
  blocking collectives: 165 us -> 0 us
  Pallas kernels: 0 us -> 129 us
  matrix products: 115 us -> 0 us
  other arithmetic: 17.6 us -> 1.58 us
  between operations: 13.9 us -> 0.72 us
  local copies, waits for them, and re-layouts: 1.17 us -> 7.97 us
    psum x4 -> x0, waiting for transfers between devices: 212 us -> none  [the longest x2 173 us: body(): raw_sums = lax.psum(right_partial, 'row')]
    psum x4 -> x0, blocking collectives: 165 us -> none  [the longest x2 158 us: body(): totals = lax.psum(squares, 'row')]
    pallas_call x0 -> x1, Pallas kernels: none -> 129 us  [fused(): pl.pallas_call(functools.partial(kernel, sizes, rows, probes), out_shape=...]
    dot_general x12 -> x0, matrix products: 115 us -> none  [the longest x6 57.4 us: body(): jnp.einsum('lmoi,lmki->lmko', weight, vector, preferred_element_type=jnp....]
    reduce_sum x11 -> x0, other arithmetic: 9.23 us -> none  [the longest x5 8.61 us: body(): jnp.sum(piece * piece, axis=3)]
  transfers between devices with their start and end apart: 4 -> 0, of which waited for: 4 -> 0; matrix products, arithmetic and copies ran while one was open for 0% -> 0% of each run, Pallas kernels for 0% -> 0%
where the time goes in v1:
time: 140 us
  Pallas kernels  129 us (92%)
  local copies, waits for them, and re-layouts  7.97 us (6%)
  other arithmetic  1.58 us (1%)
    pallas_call x1, Pallas kernels, fused(): pl.pallas_call(functools.partial(kernel, sizes, rows, probes), out_shape=...  129 us
    reshape x3, local copies, waits for them, and re-layouts, fused(): outs.append(value.transpose(0, 2, 1, 3).reshape(start.shape))  3.63 us

profile of v1, /device:TPU:0, one launch (start us, length us, event | category | flops | bytes accessed | tf_op | source)
XLA Modules:
  0.0 139.7 jit_solution(5501207507168477564)
XLA Ops:
  0.6 129.5 %shard_map.109 = (bf16[4,16,16,256]{3,2,1,0:T(8,128)(2,1)}, bf16[2,16,16,896]{3,2,1,0:T(8,128)(2,1)}, bf16[4,16,16,256]{3,2,1,0:T(8,128)(2,1)}, f32[16,128]{1,0:T(8,128)}, f32[16,128]{1,0:T(8,128)}) custom-call(bf16[8,896,2048]{2,1,0:T(8,128)(2,1)} %bitcast.36, bf16[4,256,7168]{2,1,0:T(8,128)(2,1)} %refs_1_.1, bf16[8,256,2048]{2,1,0:T(8,128)(2,1)} %bitcast.37, ...), custom_call_target="tpu_custom_call" | custom-call | flops 3355443200 | bytes 52428800 | tf_op jit(solution)/shard_map/pallas_call | solution.py:352
  130.1 0.8 slice_bitcast_fusion
  130.9 0.1 copy.12
  131.0 1.2 fusion.2
  132.2 0.0 copy-start.2
  132.2 0.0 copy-start.3
  132.2 0.0 copy-start
  132.2 0.6 copy.13
  132.9 1.1 reshape.55
  134.0 0.0 copy-done.2
  134.0 0.0 copy-done.3
  134.0 0.1 slice_bitcast_fusion.1
  134.1 0.1 copy.14
  134.2 0.0 copy-done
  134.2 0.2 fusion
  134.4 0.0 copy-start.1
  134.4 1.4 copy.21
  135.8 0.1 copy.16
  135.8 0.0 copy-done.1
  135.8 0.2 fusion.1
  136.0 0.6 copy.17
  136.6 1.1 reshape.57
  137.7 0.7 copy.18
  138.4 0.7 copy.20
  139.1 0.7 copy.19
Async XLA Ops:
  132.2 1.8 %copy-start.2 = (f32[16,128]{1,0:T(8,128)S(1)}, f32[16,128]{1,0:T(8,128)}, u32[]{:S(2)}) copy-start(f32[16,128]{1,0:T(8,128)} %get-tuple-element.12) | copy-start | bytes 24580
  132.2 1.8 %copy-start.3 = (f32[16,128]{1,0:T(8,128)S(1)}, f32[16,128]{1,0:T(8,128)}, u32[]{:S(2)}) copy-start(f32[16,128]{1,0:T(8,128)} %get-tuple-element.15) | copy-start | bytes 24580
  132.2 1.9 %copy-start = (bf16[2,16,16,896]{3,2,1,0:T(8,128)(2,1)S(1)}, bf16[2,16,16,896]{3,2,1,0:T(8,128)(2,1)}, u32[]{:S(2)}) copy-start(bf16[2,16,16,896]{3,2,1,0:T(8,128)(2,1)} %get-tuple-element.13) | copy-start | bytes 2752516
  134.4 1.4 %copy-start.1 = (bf16[4,16,16,256]{3,2,1,0:T(8,128)(2,1)S(1)}, bf16[4,16,16,256]{3,2,1,0:T(8,128)(2,1)}, u32[]{:S(2)}) copy-start(bf16[4,16,16,256]{3,2,1,0:T(8,128)(2,1)} %get-tuple-element.14) | copy-start | bytes 1572868

commit v2 on v1

--- a/solution.py
+++ b/solution.py
@@ -238,7 +238,7 @@
         rtc[col] = jnp.zeros((probes, LANES), jnp.float32)
         left_ref[...] = jnp.zeros_like(left_ref)
         count = len(order)
-        for step in range(count + 5):
+        for step in range(count + 7):
             if step < count:
                 stage_left(turn, *order[step])
             if 0 <= step - 1 < count:
@@ -249,7 +249,7 @@
                     left_plane(k).start()
             if 0 <= step - 3 < count:
                 stage_plane(*order[step - 3])
-            if step == count + 2:
+            if step == count + 3:
                 for q in plane:
                     pltpu.make_async_copy(ltp.at[q], ltp.at[q], ltsem.at[1, q]).wait()
                 total = ltp[0]
@@ -258,10 +258,10 @@
                 ltl[high] = total
                 for k in range(high_n - 1):
                     left_line(k).start()
-            if 0 <= step - 4 < count:
-                stage_line(*order[step - 4])
             if 0 <= step - 5 < count:
-                stage_spread(*order[step - 5])
+                stage_line(*order[step - 5])
+            if 0 <= step - 7 < count:
+                stage_spread(*order[step - 7])
         for g, b in order:
             stage_last(g, b)
         right_across().start()

time: 140 us -> 134 us (0.957)
  Pallas kernels: 129 us -> 124 us
    pallas_call x1, Pallas kernels: 129 us -> 124 us  [fused(): pl.pallas_call(functools.partial(kernel, sizes, rows, probes), out_shape=...]
where the time goes in v2:
time: 134 us
  Pallas kernels  124 us (93%)
  local copies, waits for them, and re-layouts  7.97 us (6%)
  other arithmetic  1.58 us (1%)
    pallas_call x1, Pallas kernels, fused(): pl.pallas_call(functools.partial(kernel, sizes, rows, probes), out_shape=...  124 us
    reshape x3, local copies, waits for them, and re-layouts, fused(): outs.append(value.transpose(0, 2, 1, 3).reshape(start.shape))  3.63 us

profile of v2, /device:TPU:0, one launch (start us, length us, event | category | flops | bytes accessed | tf_op | source)
XLA Modules:
  0.0 134.2 jit_solution(9747945314967178652)
XLA Ops:
  0.6 123.9 %shard_map.109 = (bf16[4,16,16,256]{3,2,1,0:T(8,128)(2,1)}, bf16[2,16,16,896]{3,2,1,0:T(8,128)(2,1)}, bf16[4,16,16,256]{3,2,1,0:T(8,128)(2,1)}, f32[16,128]{1,0:T(8,128)}, f32[16,128]{1,0:T(8,128)}) custom-call(bf16[8,896,2048]{2,1,0:T(8,128)(2,1)} %bitcast.36, bf16[4,256,7168]{2,1,0:T(8,128)(2,1)} %refs_1_.1, bf16[8,256,2048]{2,1,0:T(8,128)(2,1)} %bitcast.37, ...), custom_call_target="tpu_custom_call" | custom-call | flops 3355443200 | bytes 52428800 | tf_op jit(solution)/shard_map/pallas_call | solution.py:352
  124.5 0.8 slice_bitcast_fusion
  125.4 0.1 copy.12
  125.5 1.2 fusion.2
  126.7 0.0 copy-start.2
  126.7 0.0 copy-start.3
  126.7 0.0 copy-start
  126.7 0.6 copy.13
  127.3 1.1 reshape.55
  128.4 0.0 copy-done.2
  128.4 0.0 copy-done.3
  128.4 0.1 slice_bitcast_fusion.1
  128.5 0.1 copy.14
  128.6 0.0 copy-done
  128.6 0.2 fusion
  128.8 0.0 copy-start.1
  128.8 1.4 %copy.21 = f32[4,8,2,8,896]{4,3,1,2,0:T(8,128)} copy(f32[4,8,2,8,896]{4,3,2,1,0:T(8,128)S(1)} %fusion) | data formatting | bytes 3670016 | tf_op jit(solution)/shard_map/reshape | solution.py:369
  130.2 0.1 copy.16
  130.3 0.0 copy-done.1
  130.3 0.2 fusion.1
  130.4 0.6 copy.17
  131.1 1.1 reshape.57
  132.2 0.7 copy.18
  132.8 0.7 copy.20
  133.5 0.7 copy.19
Async XLA Ops:
  126.7 1.8 %copy-start.2 = (f32[16,128]{1,0:T(8,128)S(1)}, f32[16,128]{1,0:T(8,128)}, u32[]{:S(2)}) copy-start(f32[16,128]{1,0:T(8,128)} %get-tuple-element.12) | copy-start | bytes 24580
  126.7 1.8 %copy-start.3 = (f32[16,128]{1,0:T(8,128)S(1)}, f32[16,128]{1,0:T(8,128)}, u32[]{:S(2)}) copy-start(f32[16,128]{1,0:T(8,128)} %get-tuple-element.15) | copy-start | bytes 24580
  126.7 1.9 %copy-start = (bf16[2,16,16,896]{3,2,1,0:T(8,128)(2,1)S(1)}, bf16[2,16,16,896]{3,2,1,0:T(8,128)(2,1)}, u32[]{:S(2)}) copy-start(bf16[2,16,16,896]{3,2,1,0:T(8,128)(2,1)} %get-tuple-element.13) | copy-start | bytes 2752516
  128.8 1.4 %copy-start.1 = (bf16[4,16,16,256]{3,2,1,0:T(8,128)(2,1)S(1)}, bf16[4,16,16,256]{3,2,1,0:T(8,128)(2,1)}, u32[]{:S(2)}) copy-start(bf16[4,16,16,256]{3,2,1,0:T(8,128)(2,1)} %get-tuple-element.14) | copy-start | bytes 1572868
